TPU v7x, 32 devices: a whole 2x2x4 slice. The times are simulated.
32 devices in a mesh: frame: 2 (over x), bx: 4 (over y, core), by: 4 (over z).
Axes of the slice: x: 2, y: 2, z: 4, core: 2. Of those that a mesh axis runs over, the one named last changes fastest.
Arguments:
- features: bfloat16 [8, 16, 64, 32, 512], P('frame', None, None, 'bx', 'by'), may hold values from -26 to 26
- voxel_embed: bfloat16 [16, 64, 32, 512], P(None, None, 'bx', 'by'), may hold values from -26 to 26
- visible: int32 [8, 16, 32, 512], P('frame', None, 'bx', 'by'), may hold values from 0 to 1, as said below
- w_query: bfloat16 [64, 64], replicated, may hold values from -0.75 to 0.75
- w_key: bfloat16 [64, 64], replicated, may hold values from -0.75 to 0.75
- w_value: bfloat16 [64, 64], replicated, may hold values from -0.75 to 0.75
- w_out: bfloat16 [64, 64], replicated, may hold values from -0.75 to 0.75
- conv_weight: bfloat16 [4, 3, 3, 3, 64, 64], replicated, may hold values from -0.21875 to 0.21875
- conv_bias: float32 [4, 64], replicated, may hold values from -1.2 to 1.2
Outputs:
- volume: bfloat16 [16, 64, 32, 512], P('frame', None, 'bx', 'by')
Inputs may be any that keep to these rules, and one draw needn't show every extreme that they name: Every voxel has visible = 1 in at least one of the 8 frames.
All inputs are finite; a program needn't handle non-finite values.
Results may differ from a plain program's by a relative error of at most 0.025.
Values may be sent and summed in bfloat16 or wider, within the bound.
A program may use at most 64 MiB of HBM per device.

v0:
```python
import functools
import itertools
import math

import jax
import jax.numpy as jnp
from jax import lax
from jax.experimental import pallas as pl
from jax.experimental.pallas import tpu as pltpu
from jax.sharding import PartitionSpec as P

MESH = pl.DeviceIdType.MESH
absent_score = -1e30


def conv_kernel(
    sizes, layers, planes, rows, ch, cols, hid_ref, w_ref, b_ref, out_ref, s3, edge_out, edge_in, send_sem, recv_sem
):
    spots = [lax.axis_index(a) for a in ("frame", "bx", "by")]
    dirs = [
        d
        for d in itertools.product((-1, 0, 1), repeat=3)
        if any(d) and all(k == 0 or n > 1 for k, n in zip(d, sizes))
    ]

    def number(d):
        return (d[0] + 1) * 9 + (d[1] + 1) * 3 + d[2] + 1

    def beside(d):
        found = None
        for k, spot, n in zip(d, spots, sizes):
            if k:
                here = spot > 0 if k < 0 else spot < n - 1
                found = here if found is None else jnp.logical_and(found, here)
        return found

    def device(d):
        return tuple(spot + k for spot, k in zip(spots, d))

    def each(act):
        for d in dirs:
            pl.when(beside(d))(functools.partial(act, d))

    def source(k, length):
        return {-1: pl.ds(1, 1), 0: pl.ds(1, length), 1: pl.ds(length, 1)}[k]

    def halo(k, length):
        return {-1: pl.ds(0, 1), 0: pl.ds(1, length), 1: pl.ds(length + 1, 1)}[k]

    def landing(p, d):
        if d[2] == 0:
            return s3.at[p, halo(d[0], planes), halo(d[1], rows), 1]
        return edge_in.at[p, 0 if d[2] < 0 else 1, d[0] + 1, d[1] + 1]

    def outgoing(p, d):
        if d[2] == 0:
            src = s3.at[p, source(d[0], planes), source(d[1], rows), 1]
        else:
            src = edge_out.at[0 if d[2] < 0 else 1]
        back = tuple(-k for k in d)
        return pltpu.make_async_remote_copy(
            src_ref=src,
            dst_ref=landing(p, back),
            send_sem=send_sem.at[number(d)],
            recv_sem=recv_sem.at[p, number(back)],
            device_id=device(d),
            device_id_type=MESH,
        )

    def incoming(p, d):
        return pltpu.make_async_remote_copy(
            src_ref=landing(p, d),
            dst_ref=landing(p, d),
            send_sem=send_sem.at[number(d)],
            recv_sem=recv_sem.at[p, number(d)],
            device_id=device(d),
            device_id_type=MESH,
        )

    zero = jnp.zeros((ch, cols), jnp.bfloat16)
    for p in range(2):
        for x in range(rows + 2):
            s3[p, 0, x, 1] = zero
            s3[p, planes + 1, x, 1] = zero
        for z in range(1, planes + 1):
            s3[p, z, 0, 1] = zero
            s3[p, z, rows + 1, 1] = zero
        edge_in[p] = jnp.zeros(edge_in.shape[1:], jnp.bfloat16)
    for z in range(planes):
        for x in range(rows):
            s3[0, z + 1, x + 1, 1] = hid_ref[z, x]

    barrier = pltpu.get_barrier_semaphore()
    each(lambda d: pl.semaphore_signal(barrier, inc=1, device_id=device(d), device_id_type=MESH))
    peers = 1
    for spot, n in zip(spots, sizes):
        peers = peers * (1 + (spot > 0).astype(jnp.int32) + (spot < n - 1).astype(jnp.int32))
    pl.semaphore_wait(barrier, peers - 1)

    lane = lax.broadcasted_iota(jnp.int32, (ch, cols), 1)
    pair = 2 if rows % 2 == 0 else 1

    def layer(l, carry):
        p = lax.rem(l, 2)

        def pack(z, held):
            low, high = held
            for x in range(rows):
                v = s3[p, z + 1, x + 1, 1].astype(jnp.float32)
                j = z * rows + x
                low = jnp.where(lane == j, pltpu.roll(v, j, 1), low)
                high = jnp.where(lane == j, pltpu.roll(v, lax.rem(j + 1, cols), 1), high)
            return low, high

        blank = jnp.zeros((ch, cols), jnp.float32)
        low, high = lax.fori_loop(0, planes, pack, (blank, blank))
        edge_out[0] = low.astype(jnp.bfloat16)
        edge_out[1] = high.astype(jnp.bfloat16)
        each(lambda d: outgoing(p, d).start())
        each(lambda d: incoming(p, d).wait_recv())

        def shift(zp, c):
            dz = (zp + planes - 1) // planes
            z = lax.rem(zp + planes - 1, planes)
            for xp in range(rows + 2):
                dx, x = (xp + rows - 1) // rows, (xp + rows - 1) % rows
                j = z * rows + x
                v = s3[p, zp, xp, 1].astype(jnp.float32)
                before = edge_in[p, 0, dz, dx].astype(jnp.float32)
                after = edge_in[p, 1, dz, dx].astype(jnp.float32)
                left = jnp.where(lane == 0, pltpu.roll(before, lax.rem(cols - j, cols), 1), pltpu.roll(v, 1, 1))
                right = jnp.where(
                    lane == cols - 1, pltpu.roll(after, cols - 1 - j, 1), pltpu.roll(v, cols - 1, 1)
                )
                s3[p, zp, xp, 0] = left.astype(jnp.bfloat16)
                s3[p, zp, xp, 2] = right.astype(jnp.bfloat16)
            return c

        lax.fori_loop(0, planes + 2, shift, 0)

        bias = b_ref[l]

        def strip(i, c):
            x0 = i * pair
            sums = {}
            for zp in range(planes + 2):
                lo, hi = max(0, zp - planes + 1), min(2, zp)
                taps = [s3[p, zp, pl.ds(x0 + k, 3)].reshape(9 * ch, cols) for k in range(pair)]
                data = jnp.concatenate(taps, axis=1) if pair > 1 else taps[0]
                part = jnp.dot(w_ref[l, lo * ch : (hi + 1) * ch], data, preferred_element_type=jnp.float32)
                for a in range(lo, hi + 1):
                    term = part[(a - lo) * ch : (a - lo + 1) * ch]
                    z = zp - a
                    sums[z] = sums[z] + term if z in sums else term
                z = zp - 2
                if z >= 0:
                    h = sums.pop(z) + bias
                    h = jnp.where(l < layers - 1, jnp.maximum(h, 0.0), h).astype(jnp.bfloat16)
                    for k in range(pair):
                        s3[1 - p, z + 1, x0 + 1 + k, 1] = h[:, k * cols : (k + 1) * cols]
            return c

        lax.fori_loop(0, rows // pair, strip, 0)
        each(lambda d: outgoing(p, d).wait_send())
        return carry

    lax.fori_loop(0, layers, layer, 0)
    for z in range(planes):
        for x in range(rows):
            out_ref[z, x] = s3[layers % 2, z + 1, x + 1, 1]


def convs(sizes, hidden, conv_weight, conv_bias):
    planes, rows, ch, cols = hidden.shape
    layers = conv_weight.shape[0]
    w = conv_weight.transpose(0, 1, 5, 2, 3, 4).reshape(layers, 3 * ch, 9 * ch)
    whole = pl.BlockSpec(memory_space=pltpu.VMEM)
    return pl.pallas_call(
        functools.partial(conv_kernel, sizes, layers, planes, rows, ch, cols),
        out_shape=jax.ShapeDtypeStruct(hidden.shape, jnp.bfloat16),
        in_specs=[whole] * 3,
        out_specs=whole,
        scratch_shapes=[
            pltpu.VMEM((2, planes + 2, rows + 2, 3, ch, cols), jnp.bfloat16),
            pltpu.VMEM((2, ch, cols), jnp.bfloat16),
            pltpu.VMEM((2, 2, 3, 3, ch, cols), jnp.bfloat16),
            pltpu.SemaphoreType.DMA((27,)),
            pltpu.SemaphoreType.DMA((2, 27)),
        ],
        compiler_params=pltpu.CompilerParams(
            collective_id=1, has_side_effects=True, vmem_limit_bytes=40 * 1024 * 1024
        ),
    )(hidden, w, conv_bias[:, :, None])


def shards(sizes, features, voxel_embed, visible, w_query, w_key, w_value, w_out, conv_weight, conv_bias):
    width = w_key.shape[0]
    query_data = jnp.einsum(
        "zcxy,cd->zdxy", voxel_embed, w_query, preferred_element_type=jnp.float32
    ).astype(jnp.bfloat16)
    key_data = jnp.einsum(
        "fzcxy,cd->fzdxy", features, w_key, preferred_element_type=jnp.float32
    ).astype(jnp.bfloat16)
    value_data = jnp.einsum(
        "fzcxy,cd->fzdxy", features, w_value, preferred_element_type=jnp.float32
    ).astype(jnp.bfloat16)
    scores = jnp.einsum(
        "zdxy,fzdxy->fzxy", query_data, key_data, preferred_element_type=jnp.float32
    ) / math.sqrt(width)
    is_seen = visible > 0
    highest = jnp.max(jnp.where(is_seen, scores, absent_score), axis=0)
    weights = jnp.where(is_seen, jnp.exp(scores - highest[None]), 0.0)
    weighted = jnp.sum(weights[:, :, None] * value_data, axis=0).astype(jnp.bfloat16)
    totals = jnp.sum(weights, axis=0).astype(jnp.bfloat16)
    groups = lax.axis_size("frame")
    got_weighted, got_totals = (
        lax.all_to_all(weighted, "frame", split_axis=0, concat_axis=0, tiled=True),
        lax.all_to_all(totals, "frame", split_axis=0, concat_axis=0, tiled=True),
    )
    got_highest = lax.all_to_all(
        highest.astype(jnp.bfloat16), "frame", split_axis=0, concat_axis=0, tiled=True
    ).astype(highest.dtype)
    planes = got_highest.shape[0] // groups
    got_weighted = got_weighted.reshape((groups, planes) + got_weighted.shape[1:])
    got_totals = got_totals.reshape((groups, planes) + got_totals.shape[1:])
    got_highest = got_highest.reshape((groups, planes) + got_highest.shape[1:])
    overall = jnp.max(got_highest, axis=0)
    factor = jnp.exp(got_highest - overall[None])
    merged = jnp.sum(factor[:, :, None] * got_weighted.astype(jnp.float32), axis=0)
    norm_sum = jnp.sum(factor * got_totals.astype(jnp.float32), axis=0)
    attended = (merged / norm_sum[:, None]).astype(jnp.bfloat16)
    hidden = jnp.einsum(
        "zcxy,cd->zxdy", attended, w_out, preferred_element_type=jnp.float32
    ).astype(jnp.bfloat16)
    return convs(sizes, hidden, conv_weight, conv_bias).transpose(0, 2, 1, 3)


def solution(mesh):
    sizes = tuple(mesh.shape[a] for a in ("frame", "bx", "by"))
    return jax.shard_map(
        functools.partial(shards, sizes),
        mesh=mesh,
        in_specs=(
            P("frame", None, None, "bx", "by"),
            P(None, None, "bx", "by"),
            P("frame", None, "bx", "by"),
            P(),
            P(),
            P(),
            P(),
            P(),
            P(),
        ),
        out_specs=P("frame", None, "bx", "by"),
        check_vma=False,
    )
```

profile of v0, /device:TPU:0, one launch (start us, length us, event | category | flops | bytes accessed | tf_op | source)
XLA Modules:
  0.0 141.1 jit_solution(4220948287359263503)
XLA Ops:
  0.0 0.0 copy-start
  0.0 0.0 copy-start.2
  0.0 1.6 %copy-done = bf16[16,64,8,128]{3,2,1,0:T(8,128)(2,1)S(1)} copy-done((bf16[16,64,8,128]{3,2,1,0:T(8,128)(2,1)S(1)}, bf16[16,64,8,128]{3,2,1,0:T(8,128)(2,1)}, u32[]{:S(2)}) %copy-start) | copy-done | bytes 2097176
  1.6 1.4 %bitcast_convert_fusion = f32[16,8,128,64]{2,3,1,0:T(8,128)S(1)} fusion(bf16[16,64,8,128]{3,2,1,0:T(8,128)(2,1)S(1)} %copy-done, bf16[64,64]{1,0:T(8,128)(2,1)} %param.12), kind=kOutput, calls=%fused_computation.8 | convolution fusion | flops 136314880 | bytes 6299648 | tf_op jit(solution)/shard_map/zcxy,cd->zdxy/dot_general | solution.py:198
  3.0 0.0 copy-done.2
  3.0 0.0 copy-start.1
  3.1 0.0 copy-start.4
  3.1 5.9 %multiply_reduce_fusion = f32[16,8,128,4]{2,1,0,3:T(8,128)S(1)} fusion(f32[16,8,128,64]{2,3,1,0:T(8,128)S(1)} %bitcast_convert_fusion, bf16[4,16,64,8,128]{4,3,2,1,0:T(8,128)(2,1)} %param.9, bf16[64,64]{1,0:T(8,128)(2,1)S(1)} %copy-done.2), kind=kOutput, calls=%fused_computation | convolution fusion | flops 553582592 | bytes 12853248 | tf_op jit(solution)/shard_map/fzcxy,cd->fzdxy/dot_general | solution.py:201
  9.0 0.0 copy-done.1
  9.0 0.1 fusion.14
  9.1 0.6 convert_element_type.57
  9.7 4.2 %all-to-all-start = ((bf16[16,8,128]{2,1,0:T(8,128)(2,1)}), bf16[16,8,128]{2,1,0:T(8,128)(2,1)S(1)}, u32[]{:S(2)}, u32[]{:S(2)}) async-start(bf16[16,8,128]{2,1,0:T(8,128)(2,1)} %convert_element_type.57), calls=%async_computation | async-start | bytes 65536 | tf_op jit(solution)/shard_map/all_to_all | solution.py:220
  13.9 0.7 fusion.22
  14.6 3.3 %all-to-all-done = bf16[16,8,128]{2,1,0:T(8,128)(2,1)S(1)} async-done(((bf16[16,8,128]{2,1,0:T(8,128)(2,1)}), bf16[16,8,128]{2,1,0:T(8,128)(2,1)S(1)}, u32[]{:S(2)}, u32[]{:S(2)}) %all-to-all-start) | async-done | bytes 32800 | tf_op jit(solution)/shard_map/all_to_all | solution.py:220
  17.8 3.3 %all-to-all-start.2 = ((bf16[16,8,128]{2,1,0:T(8,128)(2,1)}), bf16[16,8,128]{2,1,0:T(8,128)(2,1)S(1)}, u32[]{:S(2)}, u32[]{:S(2)}) async-start(bf16[16,8,128]{2,1,0:T(8,128)(2,1)} %get-tuple-element.5), calls=%async_computation.2 | async-start | bytes 65536 | tf_op jit(solution)/shard_map/all_to_all | solution.py:218
  21.1 0.0 copy-done.4
  21.1 7.9 %multiply_reduce_fusion.1 = bf16[64,16,8,128]{3,0,2,1:T(8,128)(2,1)} fusion(f32[4,16,8,128]{3,2,1,0:T(8,128)S(1)} %get-tuple-element.6, bf16[4,16,64,8,128]{4,3,2,1,0:T(8,128)(2,1)} %param.9, bf16[64,64]{1,0:T(8,128)(2,1)S(1)} %copy-done.4), kind=kOutput, calls=%fused_computation.1 | convolution fusion | flops 552599552 | bytes 10756096 | tf_op jit(solution)/shard_map/fzcxy,cd->fzdxy/dot_general | solution.py:204
  29.0 0.0 all-to-all-done.2
  29.0 4.8 %all-to-all-start.1 = ((bf16[16,64,8,128]{3,1,2,0:T(8,128)(2,1)}), bf16[16,64,8,128]{3,1,2,0:T(8,128)(2,1)}, u32[]{:S(2)}, u32[]{:S(2)}) async-start(bf16[16,64,8,128]{3,1,2,0:T(8,128)(2,1)} %bitcast.45), calls=%async_computation.1 | async-start | bytes 4194304 | tf_op jit(solution)/shard_map/all_to_all | solution.py:217
  33.8 0.0 copy-start.3
  33.8 5.2 %copy.28 = bf16[4,3,64,3,3,64]{5,4,3,2,1,0:T(4,128)(2,1)} copy(bf16[4,3,64,3,3,64]{2,5,4,3,1,0:T(8,128)(2,1)} %bitcast.46) | data formatting | bytes 1769472 | tf_op jit(solution)/shard_map/transpose | solution.py:176
  39.0 0.0 copy-start.5
  39.0 4.1 %reshape.27.w_ref = bf16[4,192,576]{2,1,0:T(8,128)(2,1)S(1)} reshape(bf16[4,3,64,3,3,64]{5,4,3,2,1,0:T(4,128)(2,1)} %copy.28) | data formatting | bytes 1769472 | tf_op jit(solution)/shard_map/reshape | solution.py:176
  43.1 0.0 copy-done.3
  43.1 0.1 copy.29.b_ref
  43.3 14.8 %all-to-all-done.1 = bf16[16,64,8,128]{3,1,2,0:T(8,128)(2,1)} async-done(((bf16[16,64,8,128]{3,1,2,0:T(8,128)(2,1)}), bf16[16,64,8,128]{3,1,2,0:T(8,128)(2,1)}, u32[]{:S(2)}, u32[]{:S(2)}) %all-to-all-start.1) | async-done | bytes 2097184 | tf_op jit(solution)/shard_map/all_to_all | solution.py:217
  58.1 2.6 %fusion.4 = f32[8,64,8,128]{3,1,2,0:T(8,128)S(1)} fusion(bf16[2,8,64,8,128]{4,2,3,1,0:T(8,128)(2,1)} %bitcast.19, f32[2,8,8,128]{3,2,1,0:T(8,128)S(1)} %subtract_exponential_fusion), kind=kLoop, calls=%fused_computation.7 | loop fusion | flops 2621440 | bytes 4259840 | tf_op jit(solution)/shard_map/reduce_sum | solution.py:229
  60.7 0.0 copy-done.5
  60.7 0.5 fusion.13.hid_ref
  61.2 78.3 %shard_map.91 = bf16[8,8,64,128]{3,2,1,0:T(8,128)(2,1)S(1)} custom-call(bf16[8,8,64,128]{3,2,1,0:T(8,128)(2,1)S(1)} %fusion.13.hid_ref, bf16[4,192,576]{2,1,0:T(8,128)(2,1)S(1)} %reshape.27.w_ref, f32[4,64,1]{2,1,0:T(8,128)S(1)} %copy.29.b_ref), custom_call_target="tpu_custom_call" | custom-call | tf_op jit(solution)/shard_map/pallas_call | solution.py:178
  139.4 1.7 %copy.30 = bf16[8,64,8,128]{3,2,1,0:T(8,128)(2,1)} copy(bf16[8,64,8,128]{3,1,2,0:T(8,128)(2,1)S(1)} %bitcast.44) | data formatting | bytes 2097152 | tf_op jit(solution)/shard_map/transpose | solution.py:235
  (4 shorter events, 0.0 us)
Async XLA Ops:
  0.0 1.6 %copy-start = (bf16[16,64,8,128]{3,2,1,0:T(8,128)(2,1)S(1)}, bf16[16,64,8,128]{3,2,1,0:T(8,128)(2,1)}, u32[]{:S(2)}) copy-start(bf16[16,64,8,128]{3,2,1,0:T(8,128)(2,1)} %param.10) | copy-start | bytes 6291460
  0.0 3.0 %copy-start.2 = (bf16[64,64]{1,0:T(8,128)(2,1)S(1)}, bf16[64,64]{1,0:T(8,128)(2,1)}, u32[]{:S(2)}) copy-start(bf16[64,64]{1,0:T(8,128)(2,1)} %param.13) | copy-start | bytes 24580
  3.0 6.0 %copy-start.1 = (s32[4,16,8,128]{3,2,1,0:T(8,128)S(1)}, s32[4,16,8,128]{3,2,1,0:T(8,128)}, u32[]{:S(2)}) copy-start(s32[4,16,8,128]{3,2,1,0:T(8,128)} %param.11) | copy-start | bytes 786436
  3.1 18.1 %copy-start.4 = (bf16[64,64]{1,0:T(8,128)(2,1)S(1)}, bf16[64,64]{1,0:T(8,128)(2,1)}, u32[]{:S(2)}) copy-start(bf16[64,64]{1,0:T(8,128)(2,1)} %param.14) | copy-start | bytes 24580
  9.7 8.2 %all-to-all-start = ((bf16[16,8,128]{2,1,0:T(8,128)(2,1)}), bf16[16,8,128]{2,1,0:T(8,128)(2,1)S(1)}, u32[]{:S(2)}, u32[]{:S(2)}) async-start(bf16[16,8,128]{2,1,0:T(8,128)(2,1)} %convert_element_type.57), calls=%async_computation | async-start | bytes 65536 | tf_op jit(solution)/shard_map/all_to_all | solution.py:220
  17.8 11.1 %all-to-all-start.2 = ((bf16[16,8,128]{2,1,0:T(8,128)(2,1)}), bf16[16,8,128]{2,1,0:T(8,128)(2,1)S(1)}, u32[]{:S(2)}, u32[]{:S(2)}) async-start(bf16[16,8,128]{2,1,0:T(8,128)(2,1)} %get-tuple-element.5), calls=%async_computation.2 | async-start | bytes 65536 | tf_op jit(solution)/shard_map/all_to_all | solution.py:218
  29.0 29.1 %all-to-all-start.1 = ((bf16[16,64,8,128]{3,1,2,0:T(8,128)(2,1)}), bf16[16,64,8,128]{3,1,2,0:T(8,128)(2,1)}, u32[]{:S(2)}, u32[]{:S(2)}) async-start(bf16[16,64,8,128]{3,1,2,0:T(8,128)(2,1)} %bitcast.45), calls=%async_computation.1 | async-start | bytes 4194304 | tf_op jit(solution)/shard_map/all_to_all | solution.py:217
  33.8 9.3 %copy-start.3 = (f32[4,64]{1,0:T(4,128)S(1)}, f32[4,64]{1,0:T(4,128)}, u32[]{:S(2)}) copy-start(f32[4,64]{1,0:T(4,128)} %param.17) | copy-start | bytes 3076
  39.0 21.7 %copy-start.5 = (bf16[64,64]{1,0:T(8,128)(2,1)S(1)}, bf16[64,64]{1,0:T(8,128)(2,1)}, u32[]{:S(2)}) copy-start(bf16[64,64]{1,0:T(8,128)(2,1)} %param.15) | copy-start | bytes 24580
where the time goes:
time: 142 us; the launch traced here: 141 us
  Pallas kernels  78.3 us (55%)
  waiting for transfers between devices  18 us (13%)
  matrix products  15.7 us (11%)
  local copies, waits for them, and re-layouts  12.7 us (9%)
  starting transfers between devices  12.3 us (9%)
  other arithmetic  3.96 us (3%)
    pallas_call x1, Pallas kernels, convs(): pl.pallas_call(functools.partial(conv_kernel, sizes, layers, planes, rows...  78.3 us
    all_to_all x1, waiting for transfers between devices, shards(): lax.all_to_all(weighted, 'frame', split_axis=0, concat_axis=0, tiled=True)  14.8 us
    dot_general x1, matrix products, shards(): jnp.einsum('fzcxy,cd->fzdxy', features, w_value, preferred_element_type=j...  7.86 us
    dot_general x1, matrix products, shards(): jnp.einsum('fzcxy,cd->fzdxy', features, w_key, preferred_element_type=jnp...  5.92 us
    transpose x1, local copies, waits for them, and re-layouts, convs(): w = conv_weight.transpose(0, 1, 5, 2, 3, 4).reshape(layers, 3 * ch, 9 * ch)  5.19 us
    all_to_all x1, starting transfers between devices, shards(): lax.all_to_all(weighted, 'frame', split_axis=0, concat_axis=0, tiled=True)  4.8 us
    all_to_all x1, starting transfers between devices, shards(): lax.all_to_all(highest.astype(jnp.bfloat16), 'frame', split_axis=0, conca...  4.21 us
    reshape x1, local copies, waits for them, and re-layouts, convs(): w = conv_weight.transpose(0, 1, 5, 2, 3, 4).reshape(layers, 3 * ch, 9 * ch)  4.13 us
  transfers between devices with their start and end apart: 3, of which 2 were waited for; matrix products, arithmetic and copies ran while one was open for 13% of the time, Pallas kernels for 0%

commit v1 on v0

--- a/solution.py
+++ b/solution.py
@@ -37,9 +37,18 @@
     def device(d):
         return tuple(spot + k for spot, k in zip(spots, d))
 
-    def each(act):
-        for d in dirs:
+    def each(act, some=lambda d: True):
+        for d in filter(some, dirs):
             pl.when(beside(d))(functools.partial(act, d))
+
+    def flat(d):
+        return d[2] == 0
+
+    def column(d):
+        return d[2] != 0
+
+    def straight(d):
+        return d[:2] == (0, 0)
 
     def source(k, length):
         return {-1: pl.ds(1, 1), 0: pl.ds(1, length), 1: pl.ds(length, 1)}[k]
@@ -112,17 +121,18 @@
                 high = jnp.where(lane == j, pltpu.roll(v, lax.rem(j + 1, cols), 1), high)
             return low, high
 
+        each(lambda d: outgoing(p, d).start(), flat)
         blank = jnp.zeros((ch, cols), jnp.float32)
         low, high = lax.fori_loop(0, planes, pack, (blank, blank))
         edge_out[0] = low.astype(jnp.bfloat16)
         edge_out[1] = high.astype(jnp.bfloat16)
-        each(lambda d: outgoing(p, d).start())
-        each(lambda d: incoming(p, d).wait_recv())
-
-        def shift(zp, c):
+        each(lambda d: outgoing(p, d).start(), straight)
+        each(lambda d: outgoing(p, d).start(), lambda d: column(d) and not straight(d))
+
+        def shift(xps, zp, c):
             dz = (zp + planes - 1) // planes
             z = lax.rem(zp + planes - 1, planes)
-            for xp in range(rows + 2):
+            for xp in xps:
                 dx, x = (xp + rows - 1) // rows, (xp + rows - 1) % rows
                 j = z * rows + x
                 v = s3[p, zp, xp, 1].astype(jnp.float32)
@@ -136,7 +146,11 @@
                 s3[p, zp, xp, 2] = right.astype(jnp.bfloat16)
             return c
 
-        lax.fori_loop(0, planes + 2, shift, 0)
+        each(lambda d: incoming(p, d).wait_recv(), straight)
+        lax.fori_loop(1, planes + 1, functools.partial(shift, range(1, rows + 1)), 0)
+        each(lambda d: incoming(p, d).wait_recv(), lambda d: not straight(d))
+        lax.fori_loop(1, planes + 1, functools.partial(shift, (0, rows + 1)), 0)
+        lax.fori_loop(0, 2, lambda k, c: shift(range(rows + 2), k * (planes + 1), c), 0)
 
         bias = b_ref[l]
 
@@ -213,17 +227,11 @@
     weighted = jnp.sum(weights[:, :, None] * value_data, axis=0).astype(jnp.bfloat16)
     totals = jnp.sum(weights, axis=0).astype(jnp.bfloat16)
     groups = lax.axis_size("frame")
-    got_weighted, got_totals = (
-        lax.all_to_all(weighted, "frame", split_axis=0, concat_axis=0, tiled=True),
-        lax.all_to_all(totals, "frame", split_axis=0, concat_axis=0, tiled=True),
-    )
-    got_highest = lax.all_to_all(
-        highest.astype(jnp.bfloat16), "frame", split_axis=0, concat_axis=0, tiled=True
-    ).astype(highest.dtype)
-    planes = got_highest.shape[0] // groups
-    got_weighted = got_weighted.reshape((groups, planes) + got_weighted.shape[1:])
-    got_totals = got_totals.reshape((groups, planes) + got_totals.shape[1:])
-    got_highest = got_highest.reshape((groups, planes) + got_highest.shape[1:])
+    sent = jnp.concatenate([weighted, totals[:, None], highest.astype(jnp.bfloat16)[:, None]], axis=1)
+    got = lax.all_to_all(sent, "frame", split_axis=0, concat_axis=0, tiled=True)
+    got = got.reshape((groups, got.shape[0] // groups) + got.shape[1:])
+    got_weighted, got_totals = got[:, :, :width], got[:, :, width]
+    got_highest = got[:, :, width + 1].astype(jnp.float32)
     overall = jnp.max(got_highest, axis=0)
     factor = jnp.exp(got_highest - overall[None])
     merged = jnp.sum(factor[:, :, None] * got_weighted.astype(jnp.float32), axis=0)

time: 142 us -> 130 us (0.915)
  starting transfers between devices: 12.3 us -> 4.82 us
  Pallas kernels: 78.3 us -> 72.4 us
  local copies, waits for them, and re-layouts: 12.7 us -> 14.5 us
  matrix products: 15.7 us -> 14 us
  other arithmetic: 3.96 us -> 5.52 us
    all_to_all x3 -> x1, starting transfers between devices: 12.3 us -> 4.82 us  [shards(): got = lax.all_to_all(sent, 'frame', split_axis=0, concat_axis=0, tiled=True)]
    pallas_call x1, Pallas kernels: 78.3 us -> 72.4 us  [convs(): pl.pallas_call(functools.partial(conv_kernel, sizes, layers, planes, rows...]
    dot_general x1, matrix products: 7.86 us -> 6.17 us  [shards(): jnp.einsum('fzcxy,cd->fzdxy', features, w_value, preferred_element_type=j...]
    concatenate x0 -> x1, local copies, waits for them, and re-layouts: none -> 1.64 us  [shards(): jnp.concatenate([weighted, totals[:, None], highest.astype(jnp.bfloat16)[...]
    all_to_all x3 -> x1, waiting for transfers between devices: 18 us -> 17.7 us  [shards(): got = lax.all_to_all(sent, 'frame', split_axis=0, concat_axis=0, tiled=True)]
  transfers between devices with their start and end apart: 3 -> 1, of which waited for: 2 -> 1; matrix products, arithmetic and copies ran while one was open for 13% -> 7% of each run, Pallas kernels for 0% -> 0%
where the time goes in v1:
time: 130 us; the launch traced here: 129 us
  Pallas kernels  72.4 us (56%)
  waiting for transfers between devices  17.7 us (14%)
  local copies, waits for them, and re-layouts  14.5 us (11%)
  matrix products  14 us (11%)
  other arithmetic  5.52 us (4%)
  starting transfers between devices  4.82 us (4%)
    pallas_call x1, Pallas kernels, convs(): pl.pallas_call(functools.partial(conv_kernel, sizes, layers, planes, rows...  72.4 us
    all_to_all x1, waiting for transfers between devices, shards(): got = lax.all_to_all(sent, 'frame', split_axis=0, concat_axis=0, tiled=True)  17.7 us
    dot_general x1, matrix products, shards(): jnp.einsum('fzcxy,cd->fzdxy', features, w_value, preferred_element_type=j...  6.17 us
    dot_general x1, matrix products, shards(): jnp.einsum('fzcxy,cd->fzdxy', features, w_key, preferred_element_type=jnp...  5.92 us
    transpose x1, local copies, waits for them, and re-layouts, convs(): w = conv_weight.transpose(0, 1, 5, 2, 3, 4).reshape(layers, 3 * ch, 9 * ch)  5.19 us
    all_to_all x1, starting transfers between devices, shards(): got = lax.all_to_all(sent, 'frame', split_axis=0, concat_axis=0, tiled=True)  4.82 us
    reshape x1, local copies, waits for them, and re-layouts, convs(): w = conv_weight.transpose(0, 1, 5, 2, 3, 4).reshape(layers, 3 * ch, 9 * ch)  4.11 us
  transfers between devices with their start and end apart: 1, of which 1 were waited for; matrix products, arithmetic and copies ran while one was open for 7% of the time, Pallas kernels for 0%

profile of v1, /device:TPU:0, one launch (start us, length us, event | category | flops | bytes accessed | tf_op | source)
XLA Modules:
  0.0 129.1 jit_solution(13370068489298870318)
XLA Ops:
  0.0 0.0 copy-start
  0.0 1.6 %copy-done = bf16[16,64,8,128]{3,2,1,0:T(8,128)(2,1)S(1)} copy-done((bf16[16,64,8,128]{3,2,1,0:T(8,128)(2,1)S(1)}, bf16[16,64,8,128]{3,2,1,0:T(8,128)(2,1)}, u32[]{:S(2)}) %copy-start) | copy-done | bytes 2097176
  1.6 1.4 %bitcast_convert_fusion = f32[16,8,128,64]{2,3,1,0:T(8,128)S(1)} fusion(bf16[16,64,8,128]{3,2,1,0:T(8,128)(2,1)S(1)} %copy-done, bf16[64,64]{1,0:T(8,128)(2,1)} %param.12), kind=kOutput, calls=%fused_computation.8 | convolution fusion | flops 136314880 | bytes 6299648 | tf_op jit(solution)/shard_map/zcxy,cd->zdxy/dot_general | solution.py:212
  3.0 0.0 copy-done.2
  3.0 0.0 copy-start.1
  3.1 0.0 copy-start.5
  3.1 5.9 %multiply_reduce_fusion = f32[16,8,128,4]{2,1,0,3:T(8,128)S(1)} fusion(f32[16,8,128,64]{2,3,1,0:T(8,128)S(1)} %bitcast_convert_fusion, bf16[4,16,64,8,128]{4,3,2,1,0:T(8,128)(2,1)} %param.9, bf16[64,64]{1,0:T(8,128)(2,1)S(1)} %copy-done.2), kind=kOutput, calls=%fused_computation | convolution fusion | flops 553582592 | bytes 12853248 | tf_op jit(solution)/shard_map/fzcxy,cd->fzdxy/dot_general | solution.py:215
  9.0 0.0 copy-done.1
  9.0 0.1 fusion.14
  9.1 0.1 fusion.28
  9.2 0.1 copy.53
  9.2 0.1 copy.54
  9.3 0.0 copy-done.5
  9.3 6.2 %multiply_reduce_fusion.1 = bf16[64,16,8,128]{3,0,2,1:T(8,128)(2,1)S(1)} fusion(f32[4,16,8,128]{3,2,1,0:T(8,128)S(1)} %get-tuple-element.6, bf16[4,16,64,8,128]{4,3,2,1,0:T(8,128)(2,1)} %param.9, bf16[64,64]{1,0:T(8,128)(2,1)S(1)} %copy-done.5), kind=kOutput, calls=%fused_computation.1 | convolution fusion | flops 552599552 | bytes 10756096 | tf_op jit(solution)/shard_map/fzcxy,cd->fzdxy/dot_general | solution.py:218
  15.5 0.5 pad_maximum_fusion
  15.9 1.6 %copy.55 = bf16[16,66,8,128]{3,2,1,0:T(8,128)(2,1)} copy(bf16[16,66,8,128]{3,1,2,0:T(8,128)(2,1)S(1)} %pad_maximum_fusion) | data formatting | bytes 4325376 | tf_op jit(solution)/shard_map/concatenate | solution.py:230
  17.6 4.8 %all-to-all-start = ((bf16[16,66,8,128]{3,2,1,0:T(8,128)(2,1)}), bf16[16,66,8,128]{3,2,1,0:T(8,128)(2,1)}, u32[]{:S(2)}, u32[]{:S(2)}) async-start(bf16[16,66,8,128]{3,2,1,0:T(8,128)(2,1)} %copy.55), calls=%async_computation | async-start | bytes 4325376 | tf_op jit(solution)/shard_map/all_to_all | solution.py:231
  22.4 0.0 copy-start.4
  22.4 5.2 %copy.59 = bf16[4,3,64,3,3,64]{5,4,3,2,1,0:T(4,128)(2,1)} copy(bf16[4,3,64,3,3,64]{2,5,4,3,1,0:T(8,128)(2,1)} %bitcast.71) | data formatting | bytes 1769472 | tf_op jit(solution)/shard_map/transpose | solution.py:190
  27.6 4.1 %reshape.33.w_ref = bf16[4,192,576]{2,1,0:T(8,128)(2,1)S(1)} reshape(bf16[4,3,64,3,3,64]{5,4,3,2,1,0:T(4,128)(2,1)} %copy.59) | data formatting | bytes 1769472 | tf_op jit(solution)/shard_map/reshape | solution.py:190
  31.7 0.0 copy-start.3
  31.8 0.0 copy-done.4
  31.8 0.1 copy.60.b_ref
  31.9 17.7 %all-to-all-done = bf16[16,66,8,128]{3,2,1,0:T(8,128)(2,1)} async-done(((bf16[16,66,8,128]{3,2,1,0:T(8,128)(2,1)}), bf16[16,66,8,128]{3,2,1,0:T(8,128)(2,1)}, u32[]{:S(2)}, u32[]{:S(2)}) %all-to-all-start) | async-done | bytes 2162720 | tf_op jit(solution)/shard_map/all_to_all | solution.py:231
  49.6 0.8 fusion.23
  50.3 0.8 fusion.18
  51.1 0.8 fusion.22
  51.9 2.4 %multiply_reduce_fusion.2 = f32[8,64,8,128]{3,2,1,0:T(8,128)S(1)} fusion(bf16[2,8,66,8,128]{4,3,2,1,0:T(8,128)(2,1)} %bitcast.13, f32[2,8,8,128]{3,2,1,0:T(8,128)S(1)} %fusion.18), kind=kLoop, calls=%fused_computation.6 | loop fusion | flops 2621440 | bytes 4259840 | tf_op jit(solution)/shard_map/reduce_sum | solution.py:237
  54.3 0.2 divide_convert_fusion
  54.5 0.5 fusion.12.hid_ref
  55.0 72.4 %shard_map.91 = bf16[8,8,64,128]{3,2,1,0:T(8,128)(2,1)S(1)} custom-call(bf16[8,8,64,128]{3,2,1,0:T(8,128)(2,1)S(1)} %fusion.12.hid_ref, bf16[4,192,576]{2,1,0:T(8,128)(2,1)S(1)} %reshape.33.w_ref, f32[4,64,1]{2,1,0:T(8,128)S(1)} %copy.60.b_ref), custom_call_target="tpu_custom_call" | custom-call | tf_op jit(solution)/shard_map/pallas_call | solution.py:192
  127.4 1.7 %copy.61 = bf16[8,64,8,128]{3,2,1,0:T(8,128)(2,1)} copy(bf16[8,64,8,128]{3,1,2,0:T(8,128)(2,1)S(1)} %bitcast.69) | data formatting | bytes 2097152 | tf_op jit(solution)/shard_map/transpose | solution.py:243
  (4 shorter events, 0.0 us)
Async XLA Ops:
  0.0 1.6 %copy-start = (bf16[16,64,8,128]{3,2,1,0:T(8,128)(2,1)S(1)}, bf16[16,64,8,128]{3,2,1,0:T(8,128)(2,1)}, u32[]{:S(2)}) copy-start(bf16[16,64,8,128]{3,2,1,0:T(8,128)(2,1)} %param.10) | copy-start | bytes 6291460
  0.0 3.0 %copy-start.2 = (bf16[64,64]{1,0:T(8,128)(2,1)S(1)}, bf16[64,64]{1,0:T(8,128)(2,1)}, u32[]{:S(2)}) copy-start(bf16[64,64]{1,0:T(8,128)(2,1)} %param.13) | copy-start | bytes 24580
  3.0 6.0 %copy-start.1 = (s32[4,16,8,128]{3,2,1,0:T(8,128)S(1)}, s32[4,16,8,128]{3,2,1,0:T(8,128)}, u32[]{:S(2)}) copy-start(s32[4,16,8,128]{3,2,1,0:T(8,128)} %param.11) | copy-start | bytes 786436
  3.1 6.2 %copy-start.5 = (bf16[64,64]{1,0:T(8,128)(2,1)S(1)}, bf16[64,64]{1,0:T(8,128)(2,1)}, u32[]{:S(2)}) copy-start(bf16[64,64]{1,0:T(8,128)(2,1)} %param.14) | copy-start | bytes 24580
  17.6 32.0 %all-to-all-start = ((bf16[16,66,8,128]{3,2,1,0:T(8,128)(2,1)}), bf16[16,66,8,128]{3,2,1,0:T(8,128)(2,1)}, u32[]{:S(2)}, u32[]{:S(2)}) async-start(bf16[16,66,8,128]{3,2,1,0:T(8,128)(2,1)} %copy.55), calls=%async_computation | async-start | bytes 4325376 | tf_op jit(solution)/shard_map/all_to_all | solution.py:231
  22.4 9.3 %copy-start.4 = (f32[4,64]{1,0:T(4,128)S(1)}, f32[4,64]{1,0:T(4,128)}, u32[]{:S(2)}) copy-start(f32[4,64]{1,0:T(4,128)} %param.17) | copy-start | bytes 3076
  31.7 22.7 %copy-start.3 = (bf16[64,64]{1,0:T(8,128)(2,1)S(1)}, bf16[64,64]{1,0:T(8,128)(2,1)}, u32[]{:S(2)}) copy-start(bf16[64,64]{1,0:T(8,128)(2,1)} %param.15) | copy-start | bytes 24580

commit v2 on v1

--- a/solution.py
+++ b/solution.py
@@ -14,7 +14,7 @@
 
 
 def conv_kernel(
-    sizes, layers, planes, rows, ch, cols, hid_ref, w_ref, b_ref, out_ref, s3, edge_out, edge_in, send_sem, recv_sem
+    sizes, layers, planes, rows, ch, cols, hid_ref, w_ref, b_ref, out_ref, s3, edge_out, edge_in, partial_sums, send_sem, recv_sem
 ):
     spots = [lax.axis_index(a) for a in ("frame", "bx", "by")]
     dirs = [
@@ -108,6 +108,7 @@
 
     lane = lax.broadcasted_iota(jnp.int32, (ch, cols), 1)
     pair = 2 if rows % 2 == 0 else 1
+    ends = sorted({0, planes - 1})
 
     def layer(l, carry):
         p = lax.rem(l, 2)
@@ -148,33 +149,63 @@
 
         each(lambda d: incoming(p, d).wait_recv(), straight)
         lax.fori_loop(1, planes + 1, functools.partial(shift, range(1, rows + 1)), 0)
-        each(lambda d: incoming(p, d).wait_recv(), lambda d: not straight(d))
-        lax.fori_loop(1, planes + 1, functools.partial(shift, (0, rows + 1)), 0)
-        lax.fori_loop(0, 2, lambda k, c: shift(range(rows + 2), k * (planes + 1), c), 0)
-
         bias = b_ref[l]
 
-        def strip(i, c):
-            x0 = i * pair
-            sums = {}
-            for zp in range(planes + 2):
+        def product(x0, zp, lo, hi):
+            taps = [s3[p, zp, pl.ds(x0 + k, 3)].reshape(9 * ch, cols) for k in range(pair)]
+            data = jnp.concatenate(taps, axis=1) if pair > 1 else taps[0]
+            return jnp.dot(w_ref[l, lo * ch : (hi + 1) * ch], data, preferred_element_type=jnp.float32)
+
+        def finish(x0, z, total):
+            h = total + bias
+            h = jnp.where(l < layers - 1, jnp.maximum(h, 0.0), h).astype(jnp.bfloat16)
+            for k in range(pair):
+                s3[1 - p, z + 1, x0 + 1 + k, 1] = h[:, k * cols : (k + 1) * cols]
+
+        def gather(x0, zps, sums):
+            for zp in zps:
                 lo, hi = max(0, zp - planes + 1), min(2, zp)
-                taps = [s3[p, zp, pl.ds(x0 + k, 3)].reshape(9 * ch, cols) for k in range(pair)]
-                data = jnp.concatenate(taps, axis=1) if pair > 1 else taps[0]
-                part = jnp.dot(w_ref[l, lo * ch : (hi + 1) * ch], data, preferred_element_type=jnp.float32)
+                part = product(x0, zp, lo, hi)
                 for a in range(lo, hi + 1):
                     term = part[(a - lo) * ch : (a - lo + 1) * ch]
                     z = zp - a
                     sums[z] = sums[z] + term if z in sums else term
-                z = zp - 2
-                if z >= 0:
-                    h = sums.pop(z) + bias
-                    h = jnp.where(l < layers - 1, jnp.maximum(h, 0.0), h).astype(jnp.bfloat16)
-                    for k in range(pair):
-                        s3[1 - p, z + 1, x0 + 1 + k, 1] = h[:, k * cols : (k + 1) * cols]
+                if zp >= 2 and zp - 2 not in ends:
+                    finish(x0, zp - 2, sums.pop(zp - 2))
+
+        def inner_first(i, c):
+            sums = {}
+            gather(i * pair, range(1, planes + 1), sums)
+            for n, z in enumerate(ends):
+                partial_sums[i, n] = sums[z]
             return c
 
-        lax.fori_loop(0, rows // pair, strip, 0)
+        def inner_last(i, c):
+            x0 = i * pair
+            for n, z in enumerate(ends):
+                total = partial_sums[i, n]
+                if z == 0:
+                    total = total + product(x0, 0, 0, 0)
+                if z == planes - 1:
+                    total = total + product(x0, planes + 1, 2, 2)
+                finish(x0, z, total)
+            return c
+
+        def outer(i, c):
+            sums = {}
+            gather(i * pair, range(planes + 2), sums)
+            for z in ends:
+                finish(i * pair, z, sums[z])
+            return c
+
+        strips = rows // pair
+        lax.fori_loop(1, strips - 1, inner_first, 0)
+        each(lambda d: incoming(p, d).wait_recv(), lambda d: not straight(d))
+        lax.fori_loop(1, planes + 1, functools.partial(shift, (0, rows + 1)), 0)
+        lax.fori_loop(0, 2, lambda k, c: shift(range(rows + 2), k * (planes + 1), c), 0)
+        lax.fori_loop(1, strips - 1, inner_last, 0)
+        edges = min(strips, 2)
+        lax.fori_loop(0, edges, lambda k, c: outer(k * (strips - 1), c), 0)
         each(lambda d: outgoing(p, d).wait_send())
         return carry
 
@@ -198,6 +229,7 @@
             pltpu.VMEM((2, planes + 2, rows + 2, 3, ch, cols), jnp.bfloat16),
             pltpu.VMEM((2, ch, cols), jnp.bfloat16),
             pltpu.VMEM((2, 2, 3, 3, ch, cols), jnp.bfloat16),
+            pltpu.VMEM((rows, 2, ch, 2 * cols if rows % 2 == 0 else cols), jnp.float32),
             pltpu.SemaphoreType.DMA((27,)),
             pltpu.SemaphoreType.DMA((2, 27)),
         ],
@@ -207,7 +239,7 @@
     )(hidden, w, conv_bias[:, :, None])
 
 
-def shards(sizes, features, voxel_embed, visible, w_query, w_key, w_value, w_out, conv_weight, conv_bias):
+def group_part(features, voxel_embed, visible, w_query, w_key, w_value):
     width = w_key.shape[0]
     query_data = jnp.einsum(
         "zcxy,cd->zdxy", voxel_embed, w_query, preferred_element_type=jnp.float32
@@ -226,10 +258,29 @@
     weights = jnp.where(is_seen, jnp.exp(scores - highest[None]), 0.0)
     weighted = jnp.sum(weights[:, :, None] * value_data, axis=0).astype(jnp.bfloat16)
     totals = jnp.sum(weights, axis=0).astype(jnp.bfloat16)
-    groups = lax.axis_size("frame")
-    sent = jnp.concatenate([weighted, totals[:, None], highest.astype(jnp.bfloat16)[:, None]], axis=1)
-    got = lax.all_to_all(sent, "frame", split_axis=0, concat_axis=0, tiled=True)
-    got = got.reshape((groups, got.shape[0] // groups) + got.shape[1:])
+    return jnp.concatenate([weighted, totals[:, None], highest.astype(jnp.bfloat16)[:, None]], axis=1)
+
+
+def shards(sizes, features, voxel_embed, visible, w_query, w_key, w_value, w_out, conv_weight, conv_bias):
+    width = w_key.shape[0]
+    groups = sizes[0]
+    planes = features.shape[1] // groups
+    me = lax.axis_index("frame")
+
+    def part_for(owner):
+        nonlocal features, voxel_embed, visible
+
+        def cut(array, axis):
+            return lax.dynamic_slice_in_dim(array, owner * planes, planes, axis)
+
+        return group_part(cut(features, 1), cut(voxel_embed, 0), cut(visible, 1), w_query, w_key, w_value)
+
+    got = []
+    for k in range(1, groups):
+        part = part_for(lax.rem(me + k, groups))
+        part, features, voxel_embed, visible = lax.optimization_barrier((part, features, voxel_embed, visible))
+        got.append(lax.ppermute(part, "frame", [(i, (i + k) % groups) for i in range(groups)]))
+    got = jnp.stack([part_for(me)] + got)
     got_weighted, got_totals = got[:, :, :width], got[:, :, width]
     got_highest = got[:, :, width + 1].astype(jnp.float32)
     overall = jnp.max(got_highest, axis=0)

time: 130 us -> 115 us (0.88)
  waiting for transfers between devices: 17.7 us -> 0.01 us
  local copies, waits for them, and re-layouts: 14.5 us -> 26.4 us
  Pallas kernels: 72.4 us -> 68 us
  matrix products: 14 us -> 11.8 us
  starting transfers between devices: 4.82 us -> 2.93 us
    all_to_all x1 -> x0, waiting for transfers between devices: 17.7 us -> none  [shards(): got = lax.all_to_all(sent, 'frame', split_axis=0, concat_axis=0, tiled=True)]
    optimization_barrier x0 -> x3, local copies, waits for them, and re-layouts: none -> 12.6 us  [shards(): lax.optimization_barrier((part, features, voxel_embed, visible))]
    all_to_all x1 -> x0, starting transfers between devices: 4.82 us -> none  [shards(): got = lax.all_to_all(sent, 'frame', split_axis=0, concat_axis=0, tiled=True)]
    pallas_call x1, Pallas kernels: 72.4 us -> 68 us  [convs(): pl.pallas_call(functools.partial(conv_kernel, sizes, layers, planes, rows...]
    dynamic_slice x0 -> x2, local copies, waits for them, and re-layouts: none -> 3.79 us  [cut(): return lax.dynamic_slice_in_dim(array, owner * planes, planes, axis)]
    ppermute x0 -> x1, starting transfers between devices: none -> 2.93 us  [shards(): lax.ppermute(part, 'frame', [(i, (i + k) % groups) for i in range(groups)])]
    dot_general x3 -> x6, matrix products: 13.5 us -> 10.9 us  [the longest x2 5.03 us: group_part(): jnp.einsum('fzcxy,cd->fzdxy', features, w_value, preferred_element_type=j...]
    reshape x1, local copies, waits for them, and re-layouts: 4.11 us -> 1.65 us  [convs(): w = conv_weight.transpose(0, 1, 5, 2, 3, 4).reshape(layers, 3 * ch, 9 * ch)]
  transfers between devices with their start and end apart: 1 -> 1, of which waited for: 1 -> 0; matrix products, arithmetic and copies ran while one was open for 7% -> 23% of each run, Pallas kernels for 0% -> 0%
where the time goes in v2:
time: 115 us; the launch traced here: 114 us
  Pallas kernels  68 us (59%)
  local copies, waits for them, and re-layouts  26.4 us (23%)
  matrix products  11.8 us (10%)
  other arithmetic  4.8 us (4%)
  starting transfers between devices  2.93 us (3%)
    pallas_call x1, Pallas kernels, convs(): pl.pallas_call(functools.partial(conv_kernel, sizes, layers, planes, rows...  68 us
    optimization_barrier x3, local copies, waits for them, and re-layouts, shards(): lax.optimization_barrier((part, features, voxel_embed, visible))  12.6 us
    dot_general x2, matrix products, group_part(): jnp.einsum('fzcxy,cd->fzdxy', features, w_value, preferred_element_type=j...  5.03 us
    dot_general x2, matrix products, group_part(): jnp.einsum('fzcxy,cd->fzdxy', features, w_key, preferred_element_type=jnp...  4.92 us
    transpose x1, local copies, waits for them, and re-layouts, convs(): w = conv_weight.transpose(0, 1, 5, 2, 3, 4).reshape(layers, 3 * ch, 9 * ch)  4.03 us
    dynamic_slice x2, local copies, waits for them, and re-layouts, cut(): return lax.dynamic_slice_in_dim(array, owner * planes, planes, axis)  3.79 us
    ppermute x1, starting transfers between devices, shards(): lax.ppermute(part, 'frame', [(i, (i + k) % groups) for i in range(groups)])  2.93 us
  transfers between devices with their start and end apart: 1, of which 0 were waited for; matrix products, arithmetic and copies ran while one was open for 23% of the time, Pallas kernels for 0%

profile of v2, /device:TPU:0, one launch (start us, length us, event | category | flops | bytes accessed | tf_op | source)
XLA Modules:
  0.0 114.2 jit_solution(9709428226951181090)
XLA Ops:
  0.0 1.3 %constant_dynamic-slice_fusion = bf16[8,64,8,128]{3,2,1,0:T(8,128)(2,1)S(1)} fusion(bf16[16,64,8,128]{3,2,1,0:T(8,128)(2,1)} %param.10, s32[]{:T(128)S(6)} %select_n.23), kind=kLoop, calls=%fused_computation.62 | loop fusion | bytes 2097156 | tf_op jit(solution)/shard_map/dynamic_slice | solution.py:274
  1.3 2.5 %constant_dynamic-slice_fusion.1 = bf16[4,8,64,8,128]{4,3,2,1,0:T(8,128)(2,1)S(1)} fusion(bf16[4,16,64,8,128]{4,3,2,1,0:T(8,128)(2,1)} %param.9, s32[]{:T(128)S(6)} %select_n.23), kind=kLoop, calls=%fused_computation.63 | loop fusion | bytes 8388612 | tf_op jit(solution)/shard_map/dynamic_slice | solution.py:274
  3.8 0.0 copy-start.6
  3.8 0.5 fusion.19
  4.3 0.2 copy-done.6
  4.5 1.4 %multiply_reduce_fusion.1 = f32[8,8,128,4]{2,1,0,3:T(8,128)S(1)} fusion(f32[8,8,128,64]{2,3,1,0:T(8,128)S(1)} %fusion.19, bf16[4,8,64,8,128]{4,3,2,1,0:T(8,128)(2,1)S(1)} %constant_dynamic-slice_fusion.1, bf16[64,64]{1,0:T(8,128)(2,1)S(1)} %copy-done.6), kind=kOutput, calls=%fused_computation.1 | convolution fusion | flops 276791296 | bytes 6430720 | tf_op jit(solution)/shard_map/fzcxy,cd->fzdxy/dot_general | solution.py:247
  6.1 1.4 %multiply_reduce_fusion.3 = bf16[8,8,128,64]{2,3,1,0:T(8,128)(2,1)S(1)} fusion(f32[4,8,8,128]{3,2,1,0:T(8,128)S(1)} %get-tuple-element.20, bf16[4,8,64,8,128]{4,3,2,1,0:T(8,128)(2,1)S(1)} %constant_dynamic-slice_fusion.1, bf16[64,64]{1,0:T(8,128)(2,1)S(1)} %copy-done.8), kind=kOutput, calls=%fused_computation.3 | convolution fusion | flops 276299776 | bytes 5382144 | tf_op jit(solution)/shard_map/fzcxy,cd->fzdxy/dot_general | solution.py:250
  7.6 0.0 copy-start.1
  7.6 0.2 pad_maximum_fusion
  7.8 1.1 copy.80
  8.9 2.9 %collective-permute-start = (bf16[8,66,8,128]{3,2,1,0:T(8,128)(2,1)}, bf16[8,66,8,128]{3,2,1,0:T(8,128)(2,1)}, u32[]{:S(2)}, u32[]{:S(2)}) collective-permute-start(bf16[8,66,8,128]{3,2,1,0:T(8,128)(2,1)} %copy.80), channel_id=1, source_target_pairs={{0,16},{16,0},{1,17},{17,1},{2,18},{18,2},{3,19},{19,3},{4,20},{20... | collective-permute-start | bytes 3244040 | tf_op jit(solution)/shard_map/ppermute | solution.py:282
  11.8 2.0 %copy.75 = bf16[16,64,8,128]{3,1,2,0:T(8,128)(2,1)} copy(bf16[16,64,8,128]{3,2,1,0:T(8,128)(2,1)S(1)} %copy-done.1) | data formatting | bytes 4194304 | tf_op jit(solution)/shard_map/optimization_barrier | solution.py:281
  13.8 9.5 %copy.73 = bf16[4,16,64,8,128]{4,2,3,1,0:T(8,128)(2,1)} copy(bf16[4,16,64,8,128]{4,3,2,1,0:T(8,128)(2,1)} %param.9) | data formatting | bytes 16777216 | tf_op jit(solution)/shard_map/optimization_barrier | solution.py:281
  23.3 0.5 fusion.18
  23.8 3.5 %multiply_reduce_fusion = f32[8,8,128,4]{2,1,0,3:T(8,128)S(1)} fusion(f32[8,8,128,64]{2,3,1,0:T(8,128)S(1)} %fusion.18, bf16[4,16,64,8,128]{4,2,3,1,0:T(8,128)(2,1)} %copy.73, s32[]{:T(128)S(6)} %select_n.26, bf16[64,64]{1,0:T(8,128)(2,1)S(1)} %copy-done.6), kind=kOutput, calls=%fused_computation | convolution fusion | flops 276791296 | bytes 6430724 | tf_op jit(solution)/shard_map/fzcxy,cd->fzdxy/dot_general | solution.py:247
  27.5 4.0 %copy.85 = bf16[4,3,64,3,3,64]{5,4,3,2,1,0:T(4,128)(2,1)S(1)} copy(bf16[4,3,64,3,3,64]{2,5,4,3,1,0:T(8,128)(2,1)} %bitcast.87) | data formatting | bytes 1769472 | tf_op jit(solution)/shard_map/transpose | solution.py:221
  31.5 1.7 %reshape.47.w_ref = bf16[4,192,576]{2,1,0:T(8,128)(2,1)S(1)} reshape(bf16[4,3,64,3,3,64]{5,4,3,2,1,0:T(4,128)(2,1)S(1)} %copy.85) | data formatting | bytes 1769472 | tf_op jit(solution)/shard_map/reshape | solution.py:221
  33.2 0.8 copy.86.b_ref
  34.0 3.6 %multiply_reduce_fusion.2 = bf16[8,8,128,64]{2,3,1,0:T(8,128)(2,1)S(1)} fusion(f32[4,8,8,128]{3,2,1,0:T(8,128)S(1)} %get-tuple-element.16, bf16[4,16,64,8,128]{4,2,3,1,0:T(8,128)(2,1)} %copy.73, s32[]{:T(128)S(6)} %select_n.26, bf16[64,64]{1,0:T(8,128)(2,1)} %param.14), kind=kOutput, calls=%fused_computation.2 | convolution fusion | flops 276299776 | bytes 5390340 | tf_op jit(solution)/shard_map/fzcxy,cd->fzdxy/dot_general | solution.py:250
  37.6 0.2 maximum_bitcast_fusion
  37.9 1.4 %copy.137 = bf16[8,66,8,128]{3,1,2,0:T(8,128)(2,1)S(1)} copy(bf16[8,66,8,128]{3,2,1,0:T(8,128)(2,1)} %collective-permute-done) | data formatting | bytes 2162688 | tf_op jit(solution)/shard_map/ppermute | solution.py:282
  39.3 0.8 fusion.41
  40.1 0.7 reduce_max.34
  40.8 0.7 reduce_max.35
  41.5 0.1 subtract_exponential_fusion
  41.6 0.6 multiply_reduce_fusion.4
  42.3 0.1 copy-done.4
  42.3 0.0 copy-done.5
  42.4 1.2 %fusion.17 = bf16[8,64,8,128]{3,2,0,1:T(8,128)(2,1)S(1)} fusion(f32[8,64,8,128]{3,1,2,0:T(8,128)S(1)} %multiply_reduce_fusion.4, f32[8,8,128]{2,1,0:T(8,128)S(1)} %multiply_reduce_fusion.5), kind=kLoop, calls=%fused_computation.17 | loop fusion | flops 1048576 | bytes 3178496 | tf_op jit(solution)/shard_map/convert_element_type | solution.py:290
  43.6 0.9 fusion.20.hid_ref
  44.6 68.0 %shard_map.91 = bf16[8,8,64,128]{3,2,1,0:T(8,128)(2,1)S(1)} custom-call(bf16[8,8,64,128]{3,2,1,0:T(8,128)(2,1)S(1)} %fusion.20.hid_ref, bf16[4,192,576]{2,1,0:T(8,128)(2,1)S(1)} %reshape.47.w_ref, f32[4,64,1]{2,1,0:T(8,128)S(1)} %copy.86.b_ref), custom_call_target="tpu_custom_call" | custom-call | tf_op jit(solution)/shard_map/pallas_call | solution.py:223
  112.5 1.7 %copy.87 = bf16[8,64,8,128]{3,2,1,0:T(8,128)(2,1)} copy(bf16[8,64,8,128]{3,1,2,0:T(8,128)(2,1)S(1)} %bitcast.84) | data formatting | bytes 2097152 | tf_op jit(solution)/shard_map/transpose | solution.py:294
  (25 shorter events, 0.3 us)
Async XLA Ops:
  0.0 3.8 %copy-start = (bf16[64,64]{1,0:T(8,128)(2,1)S(1)}, bf16[64,64]{1,0:T(8,128)(2,1)}, u32[]{:S(2)}) copy-start(bf16[64,64]{1,0:T(8,128)(2,1)} %param.12) | copy-start | bytes 24580
  3.8 0.7 copy-start.6
  4.5 1.4 %copy-start.3 = (s32[4,16,8,128]{3,2,1,0:T(8,128)S(1)}, s32[4,16,8,128]{3,2,1,0:T(8,128)}, u32[]{:S(2)}) copy-start(s32[4,16,8,128]{3,2,1,0:T(8,128)} %param.11) | copy-start | bytes 786436
  4.5 1.6 %copy-start.8 = (bf16[64,64]{1,0:T(8,128)(2,1)S(1)}, bf16[64,64]{1,0:T(8,128)(2,1)}, u32[]{:S(2)}) copy-start(bf16[64,64]{1,0:T(8,128)(2,1)} %param.14) | copy-start | bytes 24580
  7.6 4.3 %copy-start.1 = (bf16[16,64,8,128]{3,2,1,0:T(8,128)(2,1)S(1)}, bf16[16,64,8,128]{3,2,1,0:T(8,128)(2,1)}, u32[]{:S(2)}) copy-start(bf16[16,64,8,128]{3,2,1,0:T(8,128)(2,1)} %param.10) | copy-start | bytes 6291460
  8.9 28.9 %collective-permute-start = (bf16[8,66,8,128]{3,2,1,0:T(8,128)(2,1)}, bf16[8,66,8,128]{3,2,1,0:T(8,128)(2,1)}, u32[]{:S(2)}, u32[]{:S(2)}) collective-permute-start(bf16[8,66,8,128]{3,2,1,0:T(8,128)(2,1)} %copy.80), channel_id=1, source_target_pairs={{0,16},{16,0},{1,17},{17,1},{2,18},{18,2},{3,19},{19,3},{4,20},{20... | collective-permute-start | bytes 3244040 | tf_op jit(solution)/shard_map/ppermute | solution.py:282
  13.8 9.5 %copy-start.2 = (bf16[16,64,8,128]{3,1,2,0:T(8,128)(2,1)S(1)}, bf16[16,64,8,128]{3,1,2,0:T(8,128)(2,1)}, u32[]{:S(2)}) copy-start(bf16[16,64,8,128]{3,1,2,0:T(8,128)(2,1)} %copy.75) | copy-start | bytes 6291460
  41.5 0.8 copy-start.4
  41.5 0.9 copy-start.5
  42.3 1.4 %copy-start.7 = (bf16[64,64]{1,0:T(8,128)(2,1)S(1)}, bf16[64,64]{1,0:T(8,128)(2,1)}, u32[]{:S(2)}) copy-start(bf16[64,64]{1,0:T(8,128)(2,1)} %param.15) | copy-start | bytes 24580

commit v3 on v2

--- a/solution.py
+++ b/solution.py
@@ -116,10 +116,10 @@
         def pack(z, held):
             low, high = held
             for x in range(rows):
-                v = s3[p, z + 1, x + 1, 1].astype(jnp.float32)
+                v = s3[p, z + 1, x + 1, 1]
                 j = z * rows + x
-                low = jnp.where(lane == j, pltpu.roll(v, j, 1), low)
-                high = jnp.where(lane == j, pltpu.roll(v, lax.rem(j + 1, cols), 1), high)
+                low = jnp.where(lane == j, turned(v, j, 1), low)
+                high = jnp.where(lane == j, turned(v, lax.rem(j + 1, cols), 1), high)
             return low, high
 
         each(lambda d: outgoing(p, d).start(), flat)
@@ -136,12 +136,12 @@
             for xp in xps:
                 dx, x = (xp + rows - 1) // rows, (xp + rows - 1) % rows
                 j = z * rows + x
-                v = s3[p, zp, xp, 1].astype(jnp.float32)
-                before = edge_in[p, 0, dz, dx].astype(jnp.float32)
-                after = edge_in[p, 1, dz, dx].astype(jnp.float32)
-                left = jnp.where(lane == 0, pltpu.roll(before, lax.rem(cols - j, cols), 1), pltpu.roll(v, 1, 1))
+                v = s3[p, zp, xp, 1]
+                before = edge_in[p, 0, dz, dx]
+                after = edge_in[p, 1, dz, dx]
+                left = jnp.where(lane == 0, turned(before, lax.rem(cols - j, cols), 1), turned(v, 1, 1))
                 right = jnp.where(
-                    lane == cols - 1, pltpu.roll(after, cols - 1 - j, 1), pltpu.roll(v, cols - 1, 1)
+                    lane == cols - 1, turned(after, cols - 1 - j, 1), turned(v, cols - 1, 1)
                 )
                 s3[p, zp, xp, 0] = left.astype(jnp.bfloat16)
                 s3[p, zp, xp, 2] = right.astype(jnp.bfloat16)
@@ -239,6 +239,10 @@
     )(hidden, w, conv_bias[:, :, None])
 
 
+def turned(v, by, axis):
+    return pltpu.roll(v, by, axis).astype(jnp.float32)
+
+
 def group_part(features, voxel_embed, visible, w_query, w_key, w_value):
     width = w_key.shape[0]
     query_data = jnp.einsum(
@@ -268,7 +272,7 @@
     me = lax.axis_index("frame")
 
     def part_for(owner):
-        nonlocal features, voxel_embed, visible
+        nonlocal w_query, w_key, w_value
 
         def cut(array, axis):
             return lax.dynamic_slice_in_dim(array, owner * planes, planes, axis)
@@ -278,7 +282,7 @@
     got = []
     for k in range(1, groups):
         part = part_for(lax.rem(me + k, groups))
-        part, features, voxel_embed, visible = lax.optimization_barrier((part, features, voxel_embed, visible))
+        part, w_query, w_key, w_value = lax.optimization_barrier((part, w_query, w_key, w_value))
         got.append(lax.ppermute(part, "frame", [(i, (i + k) % groups) for i in range(groups)]))
     got = jnp.stack([part_for(me)] + got)
     got_weighted, got_totals = got[:, :, :width], got[:, :, width]

time: 115 us -> 116 us (level)
  waiting for transfers between devices: 0.01 us -> 11.8 us
  local copies, waits for them, and re-layouts: 26.4 us -> 16.9 us
  matrix products: 11.8 us -> 9.68 us
    ppermute x1, waiting for transfers between devices: 0.01 us -> 11.8 us  [shards(): lax.ppermute(part, 'frame', [(i, (i + k) % groups) for i in range(groups)])]
    optimization_barrier x3 -> x1, local copies, waits for them, and re-layouts: 12.6 us -> 1.12 us  [shards(): lax.optimization_barrier((part, w_query, w_key, w_value))]
    dot_general x2, matrix products: 4.92 us -> 2.71 us  [group_part(): jnp.einsum('fzcxy,cd->fzdxy', features, w_key, preferred_element_type=jnp...]
    dynamic_slice x2, local copies, waits for them, and re-layouts: 3.79 us -> 5.72 us  [cut(): return lax.dynamic_slice_in_dim(array, owner * planes, planes, axis)]
  transfers between devices with their start and end apart: 1 -> 1, of which waited for: 0 -> 1; matrix products, arithmetic and copies ran while one was open for 23% -> 11% of each run, Pallas kernels for 0% -> 0%
where the time goes in v3:
time: 116 us; the launch traced here: 115 us
  Pallas kernels  68.9 us (59%)
  local copies, waits for them, and re-layouts  16.9 us (15%)
  waiting for transfers between devices  11.8 us (10%)
  matrix products  9.68 us (8%)
  other arithmetic  4.8 us (4%)
  starting transfers between devices  2.93 us (3%)
    pallas_call x1, Pallas kernels, convs(): pl.pallas_call(functools.partial(conv_kernel, sizes, layers, planes, rows...  68.9 us
    ppermute x1, waiting for transfers between devices, shards(): lax.ppermute(part, 'frame', [(i, (i + k) % groups) for i in range(groups)])  11.8 us
    dynamic_slice x2, local copies, waits for them, and re-layouts, cut(): return lax.dynamic_slice_in_dim(array, owner * planes, planes, axis)  5.72 us
    dot_general x2, matrix products, group_part(): jnp.einsum('fzcxy,cd->fzdxy', features, w_value, preferred_element_type=j...  5.11 us
    transpose x1, local copies, waits for them, and re-layouts, convs(): w = conv_weight.transpose(0, 1, 5, 2, 3, 4).reshape(layers, 3 * ch, 9 * ch)  4.03 us
    ppermute x1, starting transfers between devices, shards(): lax.ppermute(part, 'frame', [(i, (i + k) % groups) for i in range(groups)])  2.93 us
    dot_general x2, matrix products, group_part(): jnp.einsum('fzcxy,cd->fzdxy', features, w_key, preferred_element_type=jnp...  2.71 us
  transfers between devices with their start and end apart: 1, of which 1 were waited for; matrix products, arithmetic and copies ran while one was open for 11% of the time, Pallas kernels for 0%

profile of v3, /device:TPU:0, one launch (start us, length us, event | category | flops | bytes accessed | tf_op | source)
XLA Modules:
  0.0 115.2 jit_solution(2648140187207239040)
XLA Ops:
  0.0 0.0 copy-start
  0.0 1.7 %constant_dynamic-slice_fusion.1 = (bf16[8,64,8,128]{3,2,1,0:T(8,128)(2,1)S(1)}, bf16[8,64,8,128]{3,2,1,0:T(8,128)(2,1)S(1)}) fusion(bf16[16,64,8,128]{3,2,1,0:T(8,128)(2,1)} %param.10, s32[]{:T(128)S(6)} %select_n.24, s32[]{:T(128)S(6)} %select_n.23), kind=kLoop, calls=%fused_computation.62 | loop fusion | bytes 4194312 | tf_op jit(solution)/shard_map/dynamic_slice | solution.py:278
  1.7 4.0 %constant_dynamic-slice_fusion = (bf16[4,8,64,8,128]{4,3,2,1,0:T(8,128)(2,1)S(1)}, bf16[4,8,64,8,128]{4,3,2,1,0:T(8,128)(2,1)S(1)}) fusion(bf16[4,16,64,8,128]{4,3,2,1,0:T(8,128)(2,1)} %param.9, s32[]{:T(128)S(6)} %select_n.23, s32[]{:T(128)S(6)} %select_n.24), kind=kLoop, calls=%fused_computation.61 | loop fusion | bytes 16777224 | tf_op jit(solution)/shard_map/dynamic_slice | solution.py:278
  5.7 0.0 copy-start.5
  5.8 0.5 fusion.18
  6.3 0.2 copy-done.5
  6.5 1.4 %multiply_reduce_fusion.1 = f32[8,8,128,4]{2,1,0,3:T(8,128)S(1)} fusion(f32[8,8,128,64]{2,3,1,0:T(8,128)S(1)} %fusion.18, bf16[4,8,64,8,128]{4,3,2,1,0:T(8,128)(2,1)S(1)} %get-tuple-element.24, bf16[64,64]{1,0:T(8,128)(2,1)S(1)} %copy-done.5), kind=kOutput, calls=%fused_computation.1 | convolution fusion | flops 276791296 | bytes 6430720 | tf_op jit(solution)/shard_map/fzcxy,cd->fzdxy/dot_general | solution.py:251
  8.1 1.4 %multiply_reduce_fusion.3 = bf16[8,8,128,64]{2,3,1,0:T(8,128)(2,1)S(1)} fusion(f32[4,8,8,128]{3,2,1,0:T(8,128)S(1)} %get-tuple-element.20, bf16[4,8,64,8,128]{4,3,2,1,0:T(8,128)(2,1)S(1)} %get-tuple-element.24, bf16[64,64]{1,0:T(8,128)(2,1)S(1)} %copy-done.7), kind=kOutput, calls=%fused_computation.3 | convolution fusion | flops 276299776 | bytes 5382144 | tf_op jit(solution)/shard_map/fzcxy,cd->fzdxy/dot_general | solution.py:254
  9.5 0.2 pad_maximum_fusion
  9.7 1.1 copy.80
  10.8 2.9 %collective-permute-start = (bf16[8,66,8,128]{3,2,1,0:T(8,128)(2,1)}, bf16[8,66,8,128]{3,2,1,0:T(8,128)(2,1)}, u32[]{:S(2)}, u32[]{:S(2)}) collective-permute-start(bf16[8,66,8,128]{3,2,1,0:T(8,128)(2,1)} %copy.80), channel_id=1, source_target_pairs={{0,16},{16,0},{1,17},{17,1},{2,18},{18,2},{3,19},{19,3},{4,20},{20... | collective-permute-start | bytes 3244040 | tf_op jit(solution)/shard_map/ppermute | solution.py:286
  13.8 0.5 fusion.20
  14.2 1.3 %multiply_reduce_fusion = f32[8,8,128,4]{2,1,0,3:T(8,128)S(1)} fusion(f32[8,8,128,64]{2,3,1,0:T(8,128)S(1)} %fusion.20, bf16[4,8,64,8,128]{4,3,2,1,0:T(8,128)(2,1)S(1)} %get-tuple-element.23, bf16[64,64]{1,0:T(8,128)(2,1)S(1)} %copy-done.5), kind=kOutput, calls=%fused_computation | convolution fusion | flops 276791296 | bytes 6430720 | tf_op jit(solution)/shard_map/fzcxy,cd->fzdxy/dot_general | solution.py:251
  15.8 4.0 %copy.85 = bf16[4,3,64,3,3,64]{5,4,3,2,1,0:T(4,128)(2,1)S(1)} copy(bf16[4,3,64,3,3,64]{2,5,4,3,1,0:T(8,128)(2,1)} %bitcast.90) | data formatting | bytes 1769472 | tf_op jit(solution)/shard_map/transpose | solution.py:221
  19.8 1.7 %reshape.47.w_ref = bf16[4,192,576]{2,1,0:T(8,128)(2,1)S(1)} reshape(bf16[4,3,64,3,3,64]{5,4,3,2,1,0:T(4,128)(2,1)S(1)} %copy.85) | data formatting | bytes 1769472 | tf_op jit(solution)/shard_map/reshape | solution.py:221
  21.5 0.8 copy.86.b_ref
  22.3 3.7 %multiply_reduce_fusion.2 = bf16[64,8,8,128]{3,0,2,1:T(8,128)(2,1)S(1)} fusion(f32[4,8,8,128]{3,2,1,0:T(8,128)S(1)} %get-tuple-element.16, bf16[4,8,64,8,128]{4,3,2,1,0:T(8,128)(2,1)} %copy-done.1, bf16[64,64]{1,0:T(8,128)(2,1)} %param.14), kind=kOutput, calls=%fused_computation.2 | convolution fusion | flops 276299776 | bytes 5382144 | tf_op jit(solution)/shard_map/fzcxy,cd->fzdxy/dot_general | solution.py:254
  25.9 0.2 maximum_bitcast_fusion
  26.2 11.8 %collective-permute-done = bf16[8,66,8,128]{3,2,1,0:T(8,128)(2,1)} collective-permute-done((bf16[8,66,8,128]{3,2,1,0:T(8,128)(2,1)}, bf16[8,66,8,128]{3,2,1,0:T(8,128)(2,1)}, u32[]{:S(2)}, u32[]{:S(2)}) %collective-permute-start) | collective-permute-done | bytes 1081376 | tf_op jit(solution)/shard_map/ppermute | solution.py:286
  38.0 1.4 %copy.149 = bf16[8,66,8,128]{3,1,2,0:T(8,128)(2,1)S(1)} copy(bf16[8,66,8,128]{3,2,1,0:T(8,128)(2,1)} %collective-permute-done) | data formatting | bytes 2162688 | tf_op jit(solution)/shard_map/ppermute | solution.py:286
  39.4 0.8 fusion.39
  40.2 0.7 reduce_max.34
  40.9 0.7 reduce_max.35
  41.6 0.1 subtract_exponential_fusion
  41.7 0.6 multiply_reduce_fusion.4
  42.4 0.0 copy-start.6
  42.4 0.1 copy-done.3
  42.4 0.0 copy-done.4
  42.5 1.2 %fusion.17 = bf16[8,64,8,128]{3,2,0,1:T(8,128)(2,1)S(1)} fusion(f32[8,64,8,128]{3,1,2,0:T(8,128)S(1)} %multiply_reduce_fusion.4, f32[8,8,128]{2,1,0:T(8,128)S(1)} %multiply_reduce_fusion.5), kind=kLoop, calls=%fused_computation.17 | loop fusion | flops 1048576 | bytes 3178496 | tf_op jit(solution)/shard_map/convert_element_type | solution.py:294
  43.7 0.9 fusion.21.hid_ref
  44.6 68.9 %shard_map.91 = bf16[8,8,64,128]{3,2,1,0:T(8,128)(2,1)S(1)} custom-call(bf16[8,8,64,128]{3,2,1,0:T(8,128)(2,1)S(1)} %fusion.21.hid_ref, bf16[4,192,576]{2,1,0:T(8,128)(2,1)S(1)} %reshape.47.w_ref, f32[4,64,1]{2,1,0:T(8,128)S(1)} %copy.86.b_ref), custom_call_target="tpu_custom_call" | custom-call | tf_op jit(solution)/shard_map/pallas_call | solution.py:223
  113.5 1.7 %copy.87 = bf16[8,64,8,128]{3,2,1,0:T(8,128)(2,1)} copy(bf16[8,64,8,128]{3,1,2,0:T(8,128)(2,1)S(1)} %bitcast.87) | data formatting | bytes 2097152 | tf_op jit(solution)/shard_map/transpose | solution.py:298
  (21 shorter events, 0.3 us)
Async XLA Ops:
  0.0 5.8 %copy-start = (bf16[64,64]{1,0:T(8,128)(2,1)S(1)}, bf16[64,64]{1,0:T(8,128)(2,1)}, u32[]{:S(2)}) copy-start(bf16[64,64]{1,0:T(8,128)(2,1)} %param.12) | copy-start | bytes 24580
  5.7 8.5 %copy-start.1 = (bf16[4,8,64,8,128]{4,3,2,1,0:T(8,128)(2,1)}, bf16[4,8,64,8,128]{4,3,2,1,0:T(8,128)(2,1)S(1)}, u32[]{:S(2)}) copy-start(bf16[4,8,64,8,128]{4,3,2,1,0:T(8,128)(2,1)S(1)} %get-tuple-element.23) | copy-start | bytes 12582916
  5.7 0.7 copy-start.5
  6.5 1.4 %copy-start.2 = (s32[4,16,8,128]{3,2,1,0:T(8,128)S(1)}, s32[4,16,8,128]{3,2,1,0:T(8,128)}, u32[]{:S(2)}) copy-start(s32[4,16,8,128]{3,2,1,0:T(8,128)} %param.11) | copy-start | bytes 786436
  6.5 1.6 %copy-start.7 = (bf16[64,64]{1,0:T(8,128)(2,1)S(1)}, bf16[64,64]{1,0:T(8,128)(2,1)}, u32[]{:S(2)}) copy-start(bf16[64,64]{1,0:T(8,128)(2,1)} %param.14) | copy-start | bytes 24580
  10.8 27.1 %collective-permute-start = (bf16[8,66,8,128]{3,2,1,0:T(8,128)(2,1)}, bf16[8,66,8,128]{3,2,1,0:T(8,128)(2,1)}, u32[]{:S(2)}, u32[]{:S(2)}) collective-permute-start(bf16[8,66,8,128]{3,2,1,0:T(8,128)(2,1)} %copy.80), channel_id=1, source_target_pairs={{0,16},{16,0},{1,17},{17,1},{2,18},{18,2},{3,19},{19,3},{4,20},{20... | collective-permute-start | bytes 3244040 | tf_op jit(solution)/shard_map/ppermute | solution.py:286
  41.6 0.8 copy-start.3
  41.6 0.9 copy-start.4
  42.4 1.4 %copy-start.6 = (bf16[64,64]{1,0:T(8,128)(2,1)S(1)}, bf16[64,64]{1,0:T(8,128)(2,1)}, u32[]{:S(2)}) copy-start(bf16[64,64]{1,0:T(8,128)(2,1)} %param.15) | copy-start | bytes 24580
